TPU v7x, 32 devices: a whole 2x2x4 slice. The times are simulated.
32 devices in a mesh: groups: 2 (over y), seq: 4 (over z), dp: 4 (over x, core).
Axes of the slice: x: 2, y: 2, z: 4, core: 2. Of those that a mesh axis runs over, the one named last changes fastest.
Arguments:
- inputs: bfloat16 [8, 65536, 512], P(('groups', 'dp'), 'seq'), parts along dimension 0, may hold values from -6 to 6
- cotangent: bfloat16 [8, 65536, 512], P(('groups', 'dp'), 'seq'), parts along dimension 0, may hold values from -6 to 6
- first_factor: bfloat16 [256, 256, 256], P('seq', 'dp'), may hold values from -0.375 to 0.375
- second_factor: bfloat16 [256, 256, 256], P('seq', 'dp'), may hold values from -0.375 to 0.375
Outputs:
- mixed_out: bfloat16 [8, 65536, 512], P(('groups', 'dp'), 'seq'), parts along dimension 0
- input_grad: bfloat16 [8, 65536, 512], P(('groups', 'dp'), 'seq'), parts along dimension 0
- first_factor_grad: bfloat16 [512, 256, 256], P(('groups', 'seq'), 'dp'), parts along dimension 0
- second_factor_grad: bfloat16 [512, 256, 256], P(('groups', 'seq'), 'dp'), parts along dimension 0
There are 2 independent parts, one for each index of `groups`. A program takes and returns all parts, laid end to end along the dimension named above; an argument that names none is the same for every part. Nothing has to cross between parts.
All inputs are finite; a program needn't handle non-finite values.
Results may differ from a plain program's by a relative error of at most 0.009.
Values may be sent and summed in bfloat16 or wider, within the bound.
A program may use at most 320 MiB of HBM per device.

v0:
```python
import math
import jax
import jax.numpy as jnp
from jax import lax
from jax.sharding import PartitionSpec as P


def silu_parts(values):
    sig = jax.nn.sigmoid(values)
    return (values * sig, sig * (1.0 + values * (1.0 - sig)))


def shards(inputs, cotangent, first_factor, second_factor):
    first_full, second_full = (
        lax.all_gather(first_factor, "dp", axis=1, tiled=True),
        lax.all_gather(second_factor, "dp", axis=1, tiled=True),
    )
    seqs_here = inputs.shape[0]
    rows_here = inputs.shape[1]
    channels = inputs.shape[2]
    blocks_here = first_full.shape[0]
    block_width = first_full.shape[1]
    columns_here = second_full.shape[0]
    second_width = second_full.shape[1]
    norm_scale = 1.0 / math.sqrt(lax.axis_size("dp") * seqs_here * channels)
    blocked = inputs.reshape(seqs_here, blocks_here, block_width, channels)
    first_out = jnp.einsum(
        "ijk,bikc->bijc", first_full, blocked, preferred_element_type=jnp.float32
    ).astype(jnp.bfloat16)
    exchanged = lax.all_to_all(first_out, "seq", split_axis=2, concat_axis=1, tiled=True)
    result = jnp.einsum(
        "jik,bkjc->bjic", second_full, exchanged, preferred_element_type=jnp.float32
    )
    mixing, exchanged = (result, exchanged)
    mixing = mixing.reshape(seqs_here, rows_here, channels)
    gate_value, gate_slope = silu_parts(inputs.astype(jnp.float32))
    outputs = (mixing * gate_value).astype(jnp.bfloat16)
    cot_f32 = cotangent.astype(jnp.float32)
    gated_cot = (
        (cot_f32 * gate_value)
        .astype(jnp.bfloat16)
        .reshape(seqs_here, columns_here, second_width, channels)
    )
    grad_two = norm_scale * jnp.einsum(
        "bjic,bkjc->jik", gated_cot, exchanged, preferred_element_type=jnp.float32
    )
    back_sent = jnp.einsum(
        "jik,bjic->bkjc", second_full, gated_cot, preferred_element_type=jnp.float32
    ).astype(jnp.bfloat16)
    back_rows = lax.all_to_all(back_sent, "seq", split_axis=1, concat_axis=2, tiled=True)
    grad_one = norm_scale * jnp.einsum(
        "bijc,bikc->ijk", back_rows, blocked, preferred_element_type=jnp.float32
    )
    local_grad = jnp.einsum(
        "ijk,bijc->bikc", first_full, back_rows, preferred_element_type=jnp.float32
    )
    input_grad = (
        local_grad.reshape(seqs_here, rows_here, channels) + cot_f32 * mixing * gate_slope
    ).astype(jnp.bfloat16)
    first_sum, second_sum = (
        lax.psum_scatter(
            grad_one.astype(jnp.bfloat16), "dp", scatter_dimension=1, tiled=True
        ).astype(jnp.float32),
        lax.psum_scatter(
            grad_two.astype(jnp.bfloat16), "dp", scatter_dimension=1, tiled=True
        ).astype(jnp.float32),
    )
    return (outputs, input_grad, first_sum.astype(jnp.bfloat16), second_sum.astype(jnp.bfloat16))


def solution(mesh):
    in_specs = (
        P(("groups", "dp"), "seq", None),
        P(("groups", "dp"), "seq", None),
        P("seq", "dp", None),
        P("seq", "dp", None),
    )
    out_specs = (
        P(("groups", "dp"), "seq", None),
        P(("groups", "dp"), "seq", None),
        P(("groups", "seq"), "dp", None),
        P(("groups", "seq"), "dp", None),
    )
    return jax.shard_map(shards, mesh=mesh, in_specs=in_specs, out_specs=out_specs, check_vma=False)
```

profile of v0, /device:TPU:0, one launch (start us, length us, event | category | flops | bytes accessed | tf_op | source)
XLA Modules:
  0.0 976.6 jit_solution(17166616666703134738)
XLA Ops:
  7.2 0.7 all-gather.3.cloned.1.call-update
  7.9 62.7 %all-gather.3.cloned.1.call-done = bf16[64,256,256]{2,1,0:T(8,128)(2,1)} async-done(((bf16[64,64,256]{2,1,0:T(8,128)(2,1)}), bf16[64,256,256]{2,1,0:T(8,128)(2,1)}) %all-gather.3.cloned.1.call-update) | async-done | bytes 8388624 | tf_op jit(solution)/shard_map/all_gather | solution.py:15
  70.6 19.3 %convert_bitcast_fusion.1 = bf16[1,64,256,512]{2,3,1,0:T(8,128)(2,1)} fusion(bf16[64,256,512]{2,1,0:T(8,128)(2,1)} %bitcast.45, bf16[64,256,256]{2,1,0:T(8,128)(2,1)} %all-gather.3.cloned.1.call-done), kind=kOutput, calls=%fused_computation.19 | convolution fusion | flops 4303355904 | bytes 41943040 | tf_op jit(solution)/shard_map/ijk,bikc->bijc/dot_general | solution.py:27
  89.9 23.4 %copy.19 = bf16[1,64,256,512]{3,1,0,2:T(8,128)(2,1)} copy(bf16[1,64,256,512]{2,3,1,0:T(8,128)(2,1)} %convert_bitcast_fusion.1) | data formatting | bytes 33554432 | tf_op jit(solution)/shard_map/convert_element_type | solution.py:29
  113.3 7.0 all-to-all-start
  120.3 0.0 all-gather.5.cloned.1.call-start
  120.3 0.7 all-gather.5.cloned.1.call-update
  121.0 22.1 %fusion = bf16[1,16384,512]{2,1,0:T(8,128)(2,1)} fusion(bf16[1,16384,512]{2,1,0:T(8,128)(2,1)} %param.5, bf16[1,16384,512]{2,1,0:T(8,128)(2,1)} %param.4), kind=kLoop, calls=%fused_computation.5 | loop fusion | flops 67108864 | bytes 50331648 | tf_op jit(solution)/shard_map/convert_element_type | solution.py:41
  143.1 38.3 %all-gather.5.cloned.1.call-done = bf16[64,256,256]{2,1,0:T(8,128)(2,1)} async-done(((bf16[64,64,256]{2,1,0:T(8,128)(2,1)}), bf16[64,256,256]{2,1,0:T(8,128)(2,1)}) %all-gather.5.cloned.1.call-update) | async-done | bytes 8388624 | tf_op jit(solution)/shard_map/all_gather | solution.py:16
  181.5 16.4 %convert_bitcast_fusion = bf16[1,256,64,512]{1,3,2,0:T(8,128)(2,1)} fusion(bf16[64,256,512]{2,1,0:T(8,128)(2,1)} %bitcast.47, bf16[64,256,256]{2,1,0:T(8,128)(2,1)} %all-gather.5.cloned.1.call-done), kind=kOutput, calls=%fused_computation.18 | convolution fusion | flops 4303355904 | bytes 41943040 | tf_op jit(solution)/shard_map/jik,bjic->bkjc/dot_general | solution.py:47
  197.9 23.4 %copy.23 = bf16[1,256,64,512]{3,2,0,1:T(8,128)(2,1)} copy(bf16[1,256,64,512]{1,3,2,0:T(8,128)(2,1)} %convert_bitcast_fusion) | data formatting | bytes 33554432 | tf_op jit(solution)/shard_map/convert_element_type | solution.py:49
  221.3 262.6 %all-to-all-done = bf16[1,64,256,512]{3,1,0,2:T(8,128)(2,1)} async-done(((bf16[1,64,256,512]{3,1,0,2:T(8,128)(2,1)}), bf16[1,64,256,512]{3,1,0,2:T(8,128)(2,1)}, u32[]{:S(2)}, u32[]{:S(2)}) %all-to-all-start) | async-done | bytes 16777248 | tf_op jit(solution)/shard_map/all_to_all | solution.py:30
  483.8 7.1 all-to-all-start.1
  490.9 0.2 reduce-scatter.5.cloned.1.call-start
  491.2 12.1 %copy.20 = bf16[1,64,256,512]{3,2,1,0:T(8,128)(2,1)S(1)} copy(bf16[1,64,256,512]{3,1,0,2:T(8,128)(2,1)} %all-to-all-done) | data formatting | bytes 33554432 | tf_op jit(solution)/shard_map/all_to_all | solution.py:30
  503.3 21.2 %copy.21 = bf16[1,4,64,64,512]{4,2,1,3,0:T(8,128)(2,1)} copy(bf16[1,4,64,64,512]{4,3,1,2,0:T(8,128)(2,1)S(1)} %bitcast.53) | data formatting | bytes 33554432 | tf_op jit(solution)/shard_map/all_to_all | solution.py:30
  524.5 15.5 %multiply_convert_fusion = bf16[64,256,256]{2,1,0:T(8,128)(2,1)} fusion(bf16[64,256,512]{2,1,0:T(8,128)(2,1)} %bitcast.48, bf16[256,64,512]{2,0,1:T(8,128)(2,1)} %bitcast.49), kind=kOutput, calls=%fused_computation.16 | convolution fusion | flops 4303355904 | bytes 41943040 | tf_op jit(solution)/shard_map/bjic,bkjc->jik/dot_general | solution.py:44
  540.0 0.3 reduce-scatter.3.cloned.1.call-start
  540.3 313.4 %all-to-all-done.1 = bf16[1,256,64,512]{3,2,0,1:T(8,128)(2,1)} async-done(((bf16[1,256,64,512]{3,2,0,1:T(8,128)(2,1)}), bf16[1,256,64,512]{3,2,0,1:T(8,128)(2,1)}, u32[]{:S(2)}, u32[]{:S(2)}) %all-to-all-start.1) | async-done | bytes 16777248 | tf_op jit(solution)/shard_map/all_to_all | solution.py:50
  853.7 14.1 %copy.24 = bf16[1,64,4,64,512]{4,3,2,1,0:T(8,128)(2,1)} copy(bf16[1,64,4,64,512]{4,3,1,2,0:T(8,128)(2,1)} %bitcast.13) | data formatting | bytes 33554432 | tf_op jit(solution)/shard_map/all_to_all | solution.py:50
  867.7 15.5 %multiply_convert_fusion.1 = bf16[64,256,256]{2,1,0:T(8,128)(2,1)} fusion(bf16[64,256,512]{2,1,0:T(8,128)(2,1)} %bitcast.51, bf16[64,256,512]{2,1,0:T(8,128)(2,1)} %bitcast.46), kind=kOutput, calls=%fused_computation.17 | convolution fusion | flops 4303355904 | bytes 41943040 | tf_op jit(solution)/shard_map/bijc,bikc->ijk/dot_general | solution.py:51
  883.2 23.1 %fusion.10 = f32[64,512,256]{1,2,0:T(8,128)} fusion(bf16[64,256,512]{2,1,0:T(8,128)(2,1)} %bitcast.52, bf16[64,256,256]{2,1,0:T(8,128)(2,1)} %all-gather.3.cloned.1.call-done), kind=kOutput, calls=%fused_computation.20 | convolution fusion | flops 4294967296 | bytes 58720256 | tf_op jit(solution)/shard_map/ijk,bijc->bikc/dot_general | solution.py:54
  906.4 18.3 %fusion.11 = f32[64,512,256]{1,2,0:T(8,128)} fusion(bf16[64,256,256]{2,1,0:T(8,128)(2,1)} %all-gather.5.cloned.1.call-done, bf16[256,64,512]{2,0,1:T(8,128)(2,1)} %bitcast.50), kind=kOutput, calls=%fused_computation.21 | convolution fusion | flops 4294967296 | bytes 58720256 | tf_op jit(solution)/shard_map/jik,bkjc->bjic/dot_general | solution.py:31
  924.7 45.3 %fusion.3 = (bf16[1,16384,512]{2,1,0:T(8,128)(2,1)}, bf16[1,16384,512]{2,1,0:T(8,128)(2,1)}) fusion(bf16[1,16384,512]{2,1,0:T(8,128)(2,1)} %param.5, bf16[1,16384,512]{2,1,0:T(8,128)(2,1)} %param.4, f32[64,512,256]{1,2,0:T(8,128)} %fusion.10, f32[64,512,256]{1,2,0:T(8,128)} %fusion.11), kind=kLoop, calls=%fused_computation.8 | loop fusion | flops 134217728 | bytes 134217728 | tf_op jit(solution)/shard_map/convert_element_type | solution.py:59
  (5 shorter events, 0.1 us)
Async XLA Ops:
  7.2 63.4 %all-gather.3.cloned.1.call-start = ((), (), s32[]{:S(2)}) async-start(), calls=%async_computation.4 | async-start | bytes 10485760 | tf_op jit(solution)/shard_map/all_gather | solution.py:15
  113.3 370.5 %all-to-all-start = ((bf16[1,64,256,512]{3,1,0,2:T(8,128)(2,1)}), bf16[1,64,256,512]{3,1,0,2:T(8,128)(2,1)}, u32[]{:S(2)}, u32[]{:S(2)}) async-start(bf16[1,64,256,512]{3,1,0,2:T(8,128)(2,1)} %copy.19), calls=%async_computation | async-start | bytes 33554432 | tf_op jit(solution)/shard_map/all_to_all | solution.py:30
  120.3 61.2 %all-gather.5.cloned.1.call-start = ((), (), s32[]{:S(2)}) async-start(), calls=%async_computation.5 | async-start | bytes 10485760 | tf_op jit(solution)/shard_map/all_gather | solution.py:16
  483.8 369.8 %all-to-all-start.1 = ((bf16[1,256,64,512]{3,2,0,1:T(8,128)(2,1)}), bf16[1,256,64,512]{3,2,0,1:T(8,128)(2,1)}, u32[]{:S(2)}, u32[]{:S(2)}) async-start(bf16[1,256,64,512]{3,2,0,1:T(8,128)(2,1)} %copy.23), calls=%async_computation.1 | async-start | bytes 33554432 | tf_op jit(solution)/shard_map/all_to_all | solution.py:50
  490.9 479.1 %reduce-scatter.5.cloned.1.call-start = ((), (), s32[]{:S(2)}) async-start(), calls=%async_computation.7 | async-start | bytes 10485760 | tf_op jit(solution)/shard_map/reduce_scatter | solution.py:64
  540.0 430.0 %reduce-scatter.3.cloned.1.call-start = ((), (), s32[]{:S(2)}) async-start(), calls=%async_computation.6 | async-start | bytes 10485760 | tf_op jit(solution)/shard_map/reduce_scatter | solution.py:61
Sparse Core Ops, SparseCore 0:
  9.6 60.9 all-gather.2
  122.7 58.7 all-gather.4
  540.2 71.9 reduce-scatter.4
  883.4 69.8 reduce-scatter.2
where the time goes:
time: 978 us; the launch traced here: 977 us
  waiting for transfers between devices  678 us (69%)
  matrix products  108 us (11%)
  local copies, waits for them, and re-layouts  94.3 us (10%)
  other arithmetic  67.4 us (7%)
  starting transfers between devices  14.6 us (1%)
  between operations  13.8 us (1%)
    all_to_all x1, waiting for transfers between devices, shards(): lax.all_to_all(back_sent, 'seq', split_axis=1, concat_axis=2, tiled=True)  313 us
    all_to_all x1, waiting for transfers between devices, shards(): lax.all_to_all(first_out, 'seq', split_axis=2, concat_axis=1, tiled=True)  263 us
    all_gather x1, waiting for transfers between devices, shards(): lax.all_gather(first_factor, 'dp', axis=1, tiled=True)  62.7 us
    convert_element_type x1, other arithmetic, shards(): input_grad = (local_grad.reshape(seqs_here, rows_here, channels) + cot_f3...  45.3 us
    all_gather x1, waiting for transfers between devices, shards(): lax.all_gather(second_factor, 'dp', axis=1, tiled=True)  38.3 us
    all_to_all x2, local copies, waits for them, and re-layouts, shards(): lax.all_to_all(first_out, 'seq', split_axis=2, concat_axis=1, tiled=True)  33.4 us
    convert_element_type x1, local copies, waits for them, and re-layouts, shards(): first_out = jnp.einsum('ijk,bikc->bijc', first_full, blocked, preferred_e...  23.4 us
    convert_element_type x1, local copies, waits for them, and re-layouts, shards(): back_sent = jnp.einsum('jik,bjic->bkjc', second_full, gated_cot, preferre...  23.4 us
  transfers between devices with their start and end apart: 6, of which 4 were waited for; matrix products, arithmetic and copies ran while one was open for 23% of the time, Pallas kernels for 0%

commit v1 on v0

--- a/solution.py
+++ b/solution.py
@@ -3,6 +3,27 @@
 import jax.numpy as jnp
 from jax import lax
 from jax.sharding import PartitionSpec as P
+
+
+def collect(x, axis, dim):
+    length, index, extent = (lax.axis_size(axis), lax.axis_index(axis), x.shape[dim])
+    right = [(i, (i + 1) % length) for i in range(length)]
+    left = [(i, (i - 1) % length) for i in range(length)]
+    filled = jnp.zeros((*x.shape[:dim], length * extent, *x.shape[dim + 1 :]), x.dtype)
+    filled = lax.dynamic_update_slice_in_dim(filled, x, index * extent, axis=dim)
+    from_left = from_right = x
+    middle = length // 2
+    for lap in range(1, middle + 1):
+        from_left = lax.ppermute(from_left, axis, right)
+        filled = lax.dynamic_update_slice_in_dim(
+            filled, from_left, (index - lap) % length * extent, axis=dim
+        )
+        if lap < length - middle:
+            from_right = lax.ppermute(from_right, axis, left)
+            filled = lax.dynamic_update_slice_in_dim(
+                filled, from_right, (index + lap) % length * extent, axis=dim
+            )
+    return filled
 
 
 def silu_parts(values):
@@ -13,7 +34,7 @@
 def shards(inputs, cotangent, first_factor, second_factor):
     first_full, second_full = (
         lax.all_gather(first_factor, "dp", axis=1, tiled=True),
-        lax.all_gather(second_factor, "dp", axis=1, tiled=True),
+        collect(second_factor, "dp", 1),
     )
     seqs_here = inputs.shape[0]
     rows_here = inputs.shape[1]

time: 978 us -> 1010 us (1.033)
  waiting for transfers between devices: 678 us -> 699 us
    all_to_all x1, waiting for transfers between devices: 263 us -> 334 us  [shards(): lax.all_to_all(first_out, 'seq', split_axis=2, concat_axis=1, tiled=True)]
    all_to_all x1, waiting for transfers between devices: 313 us -> 258 us  [shards(): lax.all_to_all(back_sent, 'seq', split_axis=1, concat_axis=2, tiled=True)]
    ppermute x0 -> x3, waiting for transfers between devices: none -> 43.8 us  [the longest x2 43.8 us: collect(): from_left = lax.ppermute(from_left, axis, right)]
    all_gather x1 -> x0, waiting for transfers between devices: 38.3 us -> none  [shards(): lax.all_gather(second_factor, 'dp', axis=1, tiled=True)]
  transfers between devices with their start and end apart: 6 -> 8, of which waited for: 4 -> 4; matrix products, arithmetic and copies ran while one was open for 23% -> 23% of each run, Pallas kernels for 0% -> 0%
where the time goes in v1:
time: 1010 us
  waiting for transfers between devices  699 us (69%)
  matrix products  107 us (11%)
  local copies, waits for them, and re-layouts  104 us (10%)
  other arithmetic  66.4 us (7%)
  starting transfers between devices  19.4 us (2%)
  between operations  13.9 us (1%)
    all_to_all x1, waiting for transfers between devices, shards(): lax.all_to_all(first_out, 'seq', split_axis=2, concat_axis=1, tiled=True)  334 us
    all_to_all x1, waiting for transfers between devices, shards(): lax.all_to_all(back_sent, 'seq', split_axis=1, concat_axis=2, tiled=True)  258 us
    all_gather x1, waiting for transfers between devices, shards(): lax.all_gather(first_factor, 'dp', axis=1, tiled=True)  61.7 us
    convert_element_type x1, other arithmetic, shards(): input_grad = (local_grad.reshape(seqs_here, rows_here, channels) + cot_f3...  45.2 us
    ppermute x2, waiting for transfers between devices, collect(): from_left = lax.ppermute(from_left, axis, right)  43.8 us
    all_to_all x2, local copies, waits for them, and re-layouts, shards(): lax.all_to_all(first_out, 'seq', split_axis=2, concat_axis=1, tiled=True)  33.3 us
    dot_general x1, matrix products, shards(): jnp.einsum('ijk,bijc->bikc', first_full, back_rows, preferred_element_typ...  23.5 us
    convert_element_type x1, local copies, waits for them, and re-layouts, shards(): first_out = jnp.einsum('ijk,bikc->bijc', first_full, blocked, preferred_e...  23.3 us
  transfers between devices with their start and end apart: 8, of which 4 were waited for; matrix products, arithmetic and copies ran while one was open for 23% of the time, Pallas kernels for 0%

profile of v1, /device:TPU:0, one launch (start us, length us, event | category | flops | bytes accessed | tf_op | source)
XLA Modules:
  0.0 1009.9 jit_solution(7565920386471684931)
XLA Ops:
  7.7 2.0 collective-permute-start.1
  9.7 43.8 %collective-permute-done = bf16[64,64,256]{2,1,0:T(8,128)(2,1)} collective-permute-done((bf16[64,64,256]{2,1,0:T(8,128)(2,1)}, bf16[64,64,256]{2,1,0:T(8,128)(2,1)}, u32[]{:S(2)}, u32[]{:S(2)}) %collective-permute-start) | collective-permute-done | bytes 2097184 | tf_op jit(solution)/shard_map/ppermute | solution.py:17
  53.5 2.5 collective-permute-start.2
  56.0 21.2 %fusion = bf16[1,16384,512]{2,1,0:T(8,128)(2,1)} fusion(bf16[1,16384,512]{2,1,0:T(8,128)(2,1)} %param.5, bf16[1,16384,512]{2,1,0:T(8,128)(2,1)} %param.4), kind=kLoop, calls=%fused_computation.5 | loop fusion | flops 67108864 | bytes 50331648 | tf_op jit(solution)/shard_map/convert_element_type | solution.py:62
  78.5 1.9 constant_dynamic-update-slice_fusion.2
  80.4 1.9 constant_dynamic-update-slice_fusion.1
  84.2 3.2 copy-done
  87.5 14.8 %convert_bitcast_fusion = bf16[1,256,64,512]{1,3,2,0:T(8,128)(2,1)} fusion(bf16[64,256,512]{2,1,0:T(8,128)(2,1)} %bitcast.47, bf16[64,256,256]{2,1,0:T(8,128)(2,1)S(1)} %constant_dynamic-update-slice_fusion), kind=kOutput, calls=%fused_computation.18 | convolution fusion | flops 4303355904 | bytes 41943040 | tf_op jit(solution)/shard_map/jik,bjic->bkjc/dot_general | solution.py:68
  102.3 23.2 %copy.23 = bf16[1,256,64,512]{3,2,0,1:T(8,128)(2,1)} copy(bf16[1,256,64,512]{1,3,2,0:T(8,128)(2,1)} %convert_bitcast_fusion) | data formatting | bytes 33554432 | tf_op jit(solution)/shard_map/convert_element_type | solution.py:70
  125.5 7.0 all-to-all-start.1
  133.2 61.7 %all-gather.2.cloned.1.call-done = bf16[64,256,256]{2,1,0:T(8,128)(2,1)} async-done(((bf16[64,64,256]{2,1,0:T(8,128)(2,1)}), bf16[64,256,256]{2,1,0:T(8,128)(2,1)}) %all-gather.2.cloned.1.call-update) | async-done | bytes 8388624 | tf_op jit(solution)/shard_map/all_gather | solution.py:36
  194.9 19.3 %convert_bitcast_fusion.1 = bf16[1,64,256,512]{2,3,1,0:T(8,128)(2,1)} fusion(bf16[64,256,512]{2,1,0:T(8,128)(2,1)} %bitcast.45, bf16[64,256,256]{2,1,0:T(8,128)(2,1)} %all-gather.2.cloned.1.call-done), kind=kOutput, calls=%fused_computation.19 | convolution fusion | flops 4303355904 | bytes 41943040 | tf_op jit(solution)/shard_map/ijk,bikc->bijc/dot_general | solution.py:48
  214.2 23.3 %copy.19 = bf16[1,64,256,512]{3,1,0,2:T(8,128)(2,1)} copy(bf16[1,64,256,512]{2,3,1,0:T(8,128)(2,1)} %convert_bitcast_fusion.1) | data formatting | bytes 33554432 | tf_op jit(solution)/shard_map/convert_element_type | solution.py:50
  237.5 258.2 %all-to-all-done.1 = bf16[1,256,64,512]{3,2,0,1:T(8,128)(2,1)} async-done(((bf16[1,256,64,512]{3,2,0,1:T(8,128)(2,1)}), bf16[1,256,64,512]{3,2,0,1:T(8,128)(2,1)}, u32[]{:S(2)}, u32[]{:S(2)}) %all-to-all-start.1) | async-done | bytes 16777248 | tf_op jit(solution)/shard_map/all_to_all | solution.py:71
  495.7 7.1 all-to-all-start
  502.8 14.1 %copy.24 = bf16[1,64,4,64,512]{4,3,2,1,0:T(8,128)(2,1)} copy(bf16[1,64,4,64,512]{4,3,1,2,0:T(8,128)(2,1)} %bitcast.13) | data formatting | bytes 33554432 | tf_op jit(solution)/shard_map/all_to_all | solution.py:71
  516.9 15.5 %multiply_convert_fusion.1 = bf16[64,256,256]{2,1,0:T(8,128)(2,1)} fusion(bf16[64,256,512]{2,1,0:T(8,128)(2,1)} %bitcast.49, bf16[64,256,512]{2,1,0:T(8,128)(2,1)} %bitcast.46), kind=kOutput, calls=%fused_computation.17 | convolution fusion | flops 4303355904 | bytes 41943040 | tf_op jit(solution)/shard_map/bijc,bikc->ijk/dot_general | solution.py:72
  532.6 334.3 %all-to-all-done = bf16[1,64,256,512]{3,1,0,2:T(8,128)(2,1)} async-done(((bf16[1,64,256,512]{3,1,0,2:T(8,128)(2,1)}), bf16[1,64,256,512]{3,1,0,2:T(8,128)(2,1)}, u32[]{:S(2)}, u32[]{:S(2)}) %all-to-all-start) | async-done | bytes 16777248 | tf_op jit(solution)/shard_map/all_to_all | solution.py:51
  867.0 12.1 %copy.20 = bf16[1,64,256,512]{3,2,1,0:T(8,128)(2,1)S(1)} copy(bf16[1,64,256,512]{3,1,0,2:T(8,128)(2,1)} %all-to-all-done) | data formatting | bytes 33554432 | tf_op jit(solution)/shard_map/all_to_all | solution.py:51
  879.1 21.2 %copy.21 = bf16[1,4,64,64,512]{4,2,1,3,0:T(8,128)(2,1)} copy(bf16[1,4,64,64,512]{4,3,1,2,0:T(8,128)(2,1)S(1)} %bitcast.53) | data formatting | bytes 33554432 | tf_op jit(solution)/shard_map/all_to_all | solution.py:51
  900.3 15.5 %multiply_convert_fusion = bf16[64,256,256]{2,1,0:T(8,128)(2,1)} fusion(bf16[64,256,512]{2,1,0:T(8,128)(2,1)} %bitcast.48, bf16[256,64,512]{2,0,1:T(8,128)(2,1)} %bitcast.51), kind=kOutput, calls=%fused_computation.16 | convolution fusion | flops 4303355904 | bytes 41943040 | tf_op jit(solution)/shard_map/bjic,bkjc->jik/dot_general | solution.py:65
  915.9 23.5 %fusion.10 = f32[64,512,256]{1,2,0:T(8,128)} fusion(bf16[64,256,512]{2,1,0:T(8,128)(2,1)} %bitcast.50, bf16[64,256,256]{2,1,0:T(8,128)(2,1)} %all-gather.2.cloned.1.call-done), kind=kOutput, calls=%fused_computation.24 | convolution fusion | flops 4294967296 | bytes 58720256 | tf_op jit(solution)/shard_map/ijk,bijc->bikc/dot_general | solution.py:75
  939.4 18.7 %fusion.11 = f32[64,512,256]{1,2,0:T(8,128)} fusion(bf16[64,256,256]{2,1,0:T(8,128)(2,1)} %copy-done, bf16[256,64,512]{2,0,1:T(8,128)(2,1)} %bitcast.52), kind=kOutput, calls=%fused_computation.25 | convolution fusion | flops 4294967296 | bytes 58720256 | tf_op jit(solution)/shard_map/jik,bkjc->bjic/dot_general | solution.py:52
  958.1 45.2 %fusion.3 = (bf16[1,16384,512]{2,1,0:T(8,128)(2,1)}, bf16[1,16384,512]{2,1,0:T(8,128)(2,1)}) fusion(bf16[1,16384,512]{2,1,0:T(8,128)(2,1)} %param.5, bf16[1,16384,512]{2,1,0:T(8,128)(2,1)} %param.4, f32[64,512,256]{1,2,0:T(8,128)} %fusion.10, f32[64,512,256]{1,2,0:T(8,128)} %fusion.11), kind=kLoop, calls=%fused_computation.8 | loop fusion | flops 134217728 | bytes 134217728 | tf_op jit(solution)/shard_map/convert_element_type | solution.py:80
  (17 shorter events, 4.7 us)
Async XLA Ops:
  7.2 71.0 %copy-start.1 = (bf16[64,64,256]{2,1,0:T(8,128)(2,1)S(1)}, bf16[64,64,256]{2,1,0:T(8,128)(2,1)}, u32[]{:S(2)}) copy-start(bf16[64,64,256]{2,1,0:T(8,128)(2,1)} %param.7) | copy-start | bytes 6291460
  7.2 46.3 %collective-permute-start = (bf16[64,64,256]{2,1,0:T(8,128)(2,1)}, bf16[64,64,256]{2,1,0:T(8,128)(2,1)}, u32[]{:S(2)}, u32[]{:S(2)}) collective-permute-start(bf16[64,64,256]{2,1,0:T(8,128)(2,1)} %param.7), channel_id=1, source_target_pairs={{0,1},{1,2},{2,3},{3,0},{4,5},{5,6},{6,7},{7,4},{8,9},{9,10},{10,1... | collective-permute-start | bytes 6291464 | tf_op jit(solution)/shard_map/ppermute | solution.py:17
  7.7 72.7 %collective-permute-start.1 = (bf16[64,64,256]{2,1,0:T(8,128)(2,1)}, bf16[64,64,256]{2,1,0:T(8,128)(2,1)}, u32[]{:S(2)}, u32[]{:S(2)}) collective-permute-start(bf16[64,64,256]{2,1,0:T(8,128)(2,1)} %param.7), channel_id=1, source_target_pairs={{0,3},{1,0},{2,1},{3,2},{4,7},{5,4},{6,5},{7,6},{8,11},{9,8},{10,9... | collective-permute-start | bytes 6291464 | tf_op jit(solution)/shard_map/ppermute | solution.py:22
  53.5 28.9 %collective-permute-start.2 = (bf16[64,64,256]{2,1,0:T(8,128)(2,1)}, bf16[64,64,256]{2,1,0:T(8,128)(2,1)}, u32[]{:S(2)}, u32[]{:S(2)}) collective-permute-start(bf16[64,64,256]{2,1,0:T(8,128)(2,1)} %collective-permute-done), channel_id=1, source_target_pairs={{0,1},{1,2},{2,3},{3,0},{4,5},{5,6},{6,7},{7,4},{8,9},{9,10},{10,1... | collective-permute-start | bytes 6291464 | tf_op jit(solution)/shard_map/ppermute | solution.py:17
  84.2 3.2 copy-start
  125.5 370.2 %all-to-all-start.1 = ((bf16[1,256,64,512]{3,2,0,1:T(8,128)(2,1)}), bf16[1,256,64,512]{3,2,0,1:T(8,128)(2,1)}, u32[]{:S(2)}, u32[]{:S(2)}) async-start(bf16[1,256,64,512]{3,2,0,1:T(8,128)(2,1)} %copy.23), calls=%async_computation.1 | async-start | bytes 33554432 | tf_op jit(solution)/shard_map/all_to_all | solution.py:71
  132.5 62.4 %all-gather.2.cloned.1.call-start = ((), (), s32[]{:S(2)}) async-start(), calls=%async_computation.4 | async-start | bytes 10485760 | tf_op jit(solution)/shard_map/all_gather | solution.py:36
  495.7 371.3 %all-to-all-start = ((bf16[1,64,256,512]{3,1,0,2:T(8,128)(2,1)}), bf16[1,64,256,512]{3,1,0,2:T(8,128)(2,1)}, u32[]{:S(2)}, u32[]{:S(2)}) async-start(bf16[1,64,256,512]{3,1,0,2:T(8,128)(2,1)} %copy.19), calls=%async_computation | async-start | bytes 33554432 | tf_op jit(solution)/shard_map/all_to_all | solution.py:51
  502.8 500.5 %reduce-scatter.3.cloned.1.call-start = ((), (), s32[]{:S(2)}) async-start(), calls=%async_computation.5 | async-start | bytes 10485760 | tf_op jit(solution)/shard_map/reduce_scatter | solution.py:82
  532.4 470.9 %reduce-scatter.5.cloned.1.call-start = ((), (), s32[]{:S(2)}) async-start(), calls=%async_computation.6 | async-start | bytes 10485760 | tf_op jit(solution)/shard_map/reduce_scatter | solution.py:85
Sparse Core Ops, SparseCore 0:
  134.9 59.9 all-gather.1
  532.5 72.9 reduce-scatter.2
  916.0 69.1 reduce-scatter.4
